TPU v7x, 32 devices: a whole 2x2x4 slice. The times are simulated.
32 devices in a mesh: grp: 2 (over x), trn: 16 (over z, y, core).
Axes of the slice: x: 2, y: 2, z: 4, core: 2. Of those that a mesh axis runs over, the one named last changes fastest.
Arguments:
- train_features: bfloat16 [2, 40960, 2048], P(None, ('grp', 'trn')), parts along dimension 1, may hold values from -6 to 6
- residual_weights: float32 [2, 40960], P(None, ('grp', 'trn')), parts along dimension 1, may hold values from 0.06 to 1, as said below
- target_features: bfloat16 [2, 512, 2048], P(None, ('grp', 'trn')), parts along dimension 1, may hold values from -0.125 to 0.125
Outputs:
- scores: bfloat16 [40960, 256], P(('grp', 'trn')), parts along dimension 0
There are 2 independent parts, one for each index of `grp`. A program takes and returns all parts, laid end to end along the dimension named above; each array names one. Nothing has to cross between parts.
Inputs may be any that keep to these rules, and one draw needn't show every extreme that they name: `residual_weights`: strictly positive weights.
All inputs are finite; a program needn't handle non-finite values.
Results may differ from a plain program's by a relative error of at most 0.0004.
Values may be sent and summed in bfloat16 or wider, within the bound.
A program may use at most 64 MiB of HBM per device.

v0:
```python
import jax
import jax.numpy as jnp
from jax import lax
from jax.sharding import PartitionSpec as P


def shards(train_features, residual_weights, target_features):
    rows = train_features.shape[1]
    ckpts = train_features.shape[0]
    raw = None
    for ckpt in range(ckpts):

        def score_one(piece, start, ckpt=ckpt):
            tile = jnp.dot(train_features[ckpt], piece.T, preferred_element_type=jnp.float32)
            return residual_weights[ckpt][:, None] * tile

        term = score_one(
            lax.all_gather(target_features[ckpt], "trn", axis=0, tiled=True), jnp.int32(0)
        )
        raw = term if raw is None else raw + term
    total_rows = rows * lax.axis_size("trn")
    squares = lax.psum(jnp.sum(raw * raw, axis=0), "trn")
    power = squares / total_rows
    return (raw / jnp.sqrt(power + 1e-06)[None, :]).astype(jnp.bfloat16)


def solution(mesh):
    return jax.shard_map(
        shards,
        mesh=mesh,
        in_specs=(
            P(None, ("grp", "trn"), None),
            P(None, ("grp", "trn")),
            P(None, ("grp", "trn"), None),
        ),
        out_specs=P(("grp", "trn"), None),
        check_vma=False,
    )
```

profile of v0, /device:TPU:0, one launch (start us, length us, event | category | flops | bytes accessed | tf_op | source)
XLA Modules:
  0.0 133.1 jit_solution(6136758854531485970)
XLA Ops:
  6.5 0.0 all-gather.7.cloned.1.call-start
  6.5 1.5 %fusion.17 = (bf16[1,16,2048]{2,1,0:T(8,128)(2,1)}, bf16[1,16,2048]{2,1,0:T(8,128)(2,1)}) fusion(bf16[2,16,2048]{2,1,0:T(8,128)(2,1)} %param.5), kind=kLoop, calls=%fused_computation.16 | loop fusion | bytes 262144 | tf_op jit(solution)/shard_map/slice | solution.py:18
  8.1 0.0 all-gather.7.cloned.1.call-update
  8.1 0.0 all-gather.5.cloned.1.call-start
  8.1 0.7 all-gather.5.cloned.1.call-update
  8.8 0.8 slice_reduce_fusion.1
  9.6 40.5 %all-gather.7.cloned.1.call-done = bf16[1,256,2048]{2,1,0:T(8,128)(2,1)} async-done(((bf16[1,16,2048]{2,1,0:T(8,128)(2,1)}), bf16[1,256,2048]{2,1,0:T(8,128)(2,1)}) %all-gather.7.cloned.1.call-update) | async-done | bytes 1048592 | tf_op jit(solution)/shard_map/all_gather | solution.py:18
  50.2 4.4 %fusion.12 = f32[1280,256]{1,0:T(8,128)S(1)} fusion(bf16[2,1280,2048]{2,1,0:T(8,128)(2,1)} %param.3, bf16[1,256,2048]{2,1,0:T(8,128)(2,1)} %all-gather.7.cloned.1.call-done, f32[1280]{0:T(1024)S(1)} %get-tuple-element.6), kind=kOutput, calls=%fused_computation.8 | convolution fusion | flops 1342504960 | bytes 7607296 | tf_op jit(solution)/shard_map/dot_general | solution.py:14
  54.6 34.7 %all-gather.5.cloned.1.call-done = bf16[1,256,2048]{2,1,0:T(8,128)(2,1)} async-done(((bf16[1,16,2048]{2,1,0:T(8,128)(2,1)}), bf16[1,256,2048]{2,1,0:T(8,128)(2,1)}) %all-gather.5.cloned.1.call-update) | async-done | bytes 1048592 | tf_op jit(solution)/shard_map/all_gather | solution.py:18
  89.2 4.5 %multiply_reduce_fusion = (f32[256]{0:T(256)S(1)}, f32[1280,256]{1,0:T(8,128)S(1)}) fusion(f32[1280,256]{1,0:T(8,128)S(1)} %fusion.12, bf16[1,256,2048]{2,1,0:T(8,128)(2,1)} %all-gather.5.cloned.1.call-done, bf16[2,1280,2048]{2,1,0:T(8,128)(2,1)} %param.3, f32[1280]{0:T(1024)S(1)} %get-tuple-element.5), kind=kOutput, calls=%fused_computation.10 | convolution fusion | flops 1343487744 | bytes 8919040 | tf_op jit(solution)/shard_map/dot_general | solution.py:14
  93.7 31.6 %psum.7 = f32[256]{0:T(256)S(1)} all-reduce(f32[256]{0:T(256)S(1)} %get-tuple-element.9), channel_id=1, replica_groups=mesh['grp'=2,'trn'=16] {'trn'}, use_global_device_ids=true, to_apply=%region_1.0 | all-reduce | flops 256 | bytes 2048 | tf_op jit(solution)/shard_map/psum | solution.py:22
  125.3 1.0 divide_convert_fusion
  (1 shorter events, 0.0 us)
Async XLA Ops:
  6.5 43.7 %all-gather.7.cloned.1.call-start = ((), (), s32[]{:S(2)}) async-start(), calls=%async_computation.1 | async-start | bytes 1114112 | tf_op jit(solution)/shard_map/all_gather | solution.py:18
  8.1 81.2 %all-gather.5.cloned.1.call-start = ((), (), s32[]{:S(2)}) async-start(), calls=%async_computation | async-start | bytes 1114112 | tf_op jit(solution)/shard_map/all_gather | solution.py:18
Sparse Core Ops, SparseCore 0:
  9.5 40.6 all-gather.6
  52.4 36.8 all-gather.4
where the time goes:
time: 133 us
  waiting for transfers between devices  75.9 us (57%)
  blocking collectives  31.6 us (24%)
  between operations  13.4 us (10%)
  matrix products  8.83 us (7%)
  local copies, waits for them, and re-layouts  2.33 us (2%)
    all_gather x2, waiting for transfers between devices, shards(): lax.all_gather(target_features[ckpt], 'trn', axis=0, tiled=True)  75.2 us
    psum x1, blocking collectives, shards(): squares = lax.psum(jnp.sum(raw * raw, axis=0), 'trn')  31.6 us
    dot_general x2, matrix products, score_one(): jnp.dot(train_features[ckpt], piece.T, preferred_element_type=jnp.float32)  8.83 us
  transfers between devices with their start and end apart: 2, of which 2 were waited for; matrix products, arithmetic and copies ran while one was open for 4% of the time, Pallas kernels for 0%

commit v1 on v0

v1 whole, which is shorter than its diff:
```python
import functools

import jax
import jax.numpy as jnp
from jax import lax
from jax.experimental import pallas as pl
from jax.experimental.pallas import tpu as pltpu
from jax.sharding import PartitionSpec as P

MESH = pl.DeviceIdType.MESH
PIECES = 4
ROW_TILE = 640


def each(low, high, body):
    if high - low <= 16:
        for i in range(low, high):
            body(i)
    else:

        @pl.loop(low, high)
        def _(i):
            body(i)


def kernel(n, train, weights, targets, out, feats, rows, weight_rows, columns, raw, sums,
           own_sem, weight_sem, load_sem, z_send, z_recv, y_send, y_recv, s_send, s_recv,
           sum_send, sum_recv):
    levels = n // 4
    me = lax.axis_index("trn")
    z, y, core = me // 4, (me // 2) % 2, me % 2
    across, sibling = z * 4 + (1 - y) * 2 + core, z * 4 + y * 2 + (1 - core)
    ckpts, count, depth = train.shape
    own = targets.shape[1]
    per_ckpt = PIECES // ckpts
    width = depth // per_ckpt
    where = [(p // per_ckpt, (p % per_ckpt) * width) for p in range(PIECES)]

    def block(zz, yy, cc, p):
        ckpt, start = where[p]
        first = pl.multiple_of((zz * 4 + yy * 2 + cc) * own, own)
        return feats.at[ckpt, pl.ds(first, own), pl.ds(start, width)]

    def piece_rows(blocks, p):
        ckpt, start = where[p]
        return feats.at[ckpt, pl.ds(0, blocks * own), pl.ds(start, width)]

    def remote(ref, device, send_sem, recv_sem):
        return pltpu.make_async_remote_copy(
            src_ref=ref, dst_ref=ref, send_sem=send_sem, recv_sem=recv_sem,
            device_id={"trn": device}, device_id_type=MESH,
        )

    mine = pl.ds(pl.multiple_of(me * own, own), own)
    own_copy = pltpu.make_async_copy(targets, feats.at[:, mine, :], own_sem)
    own_copy.start()
    weight_copy = pltpu.make_async_copy(weights, weight_rows, weight_sem)
    weight_copy.start()
    loads = []
    for p, (ckpt, start) in enumerate(where):
        part = (ckpt, slice(None), pl.ds(start, width))
        loads.append(pltpu.make_async_copy(train.at[part], rows.at[part], load_sem.at[p]))
        loads[-1].start()

    above, below = z + 1 < levels, z > 0
    onward = ((above, me + 4), (below, me - 4))

    barrier = pltpu.get_barrier_semaphore()
    for device in (across, sibling):
        pl.semaphore_signal(barrier, inc=1, device_id={"trn": device}, device_id_type=MESH)
    for there, device in onward:

        @pl.when(there)
        def _():
            pl.semaphore_signal(barrier, inc=1, device_id={"trn": device}, device_id_type=MESH)

    pl.semaphore_wait(barrier, 2 + above.astype(jnp.int32) + below.astype(jnp.int32))
    own_copy.wait()

    def pass_on(way, d, p, ref):
        there, device = onward[way]

        @pl.when(there)
        def _():
            remote(ref, device, z_send.at[way, d, p], z_recv.at[way, d + 1, p]).start()

    def to_across(way, d, p, ref):
        remote(ref, across, y_send.at[p], y_recv.at[way, d, p]).start()

    def to_sibling(p, ref):
        remote(ref, sibling, s_send.at[p], s_recv.at[p]).start()

    for p in range(PIECES):
        ref = block(z, y, core, p)
        pass_on(0, 0, p, ref)
        pass_on(1, 0, p, ref)
        to_across(0, 0, p, ref)
    for p in range(PIECES):
        to_sibling(p, block(z, y, core, p))

    weight_copy.wait()
    for ckpt in range(ckpts):
        for first in range(0, count, 128):
            line = weight_rows[ckpt:ckpt + 1, first:first + 128]
            columns[ckpt, first:first + 128, :] = jnp.broadcast_to(line, (128, 128)).T

    def origin(way, d):
        return z - d if way == 0 else z + d

    def exists(way, d):
        return origin(way, d) >= 0 if way == 0 else origin(way, d) < levels

    def from_z(d, p):
        for way in range(2):

            @pl.when(exists(way, d))
            def _():
                ref = block(origin(way, d), y, core, p)
                remote(ref, me, z_send.at[way, d, p], z_recv.at[way, d, p]).wait_recv()
                pass_on(way, d, p, ref)
                to_across(way, d, p, ref)
                to_sibling(p, ref)

    def from_across(d, p, ways=2):
        for way in range(ways):

            @pl.when(exists(way, d))
            def _():
                ref = block(origin(way, d), 1 - y, core, p)
                remote(ref, me, y_send.at[p], y_recv.at[way, d, p]).wait_recv()
                to_sibling(p, ref)

    def level(d):
        for p in range(PIECES):
            from_z(d, p)
        for p in range(PIECES):
            from_across(d - 1, p)

    if levels > 1:
        for p in range(PIECES):
            from_z(1, p)
        for p in range(PIECES):
            from_across(0, p, ways=1)
        each(2, levels, level)

    targets_all = n * own
    tile = ROW_TILE if count % ROW_TILE == 0 else count
    lanes = targets_all // 128
    squares = jnp.zeros((8, targets_all), jnp.float32)
    for p, (ckpt, start) in enumerate(where):
        from_across(levels - 1, p, ways=2 if levels > 1 else 1)
        remote(piece_rows(2 * levels, p), me, s_send.at[p], s_recv.at[p]).wait_recv()
        loads[p].wait()
        for first in range(0, count, tile):
            here = slice(first, first + tile)
            product = lax.dot_general(
                rows[ckpt, here, start:start + width], feats[ckpt, :, start:start + width],
                (((1,), (1,)), ((), ())), preferred_element_type=jnp.float32,
            )
            scale = jnp.concatenate([columns[ckpt, here, :]] * lanes, axis=1)
            value = product * scale
            if p:
                value += raw[here, :]
            raw[here, :] = value
            if p == PIECES - 1:
                squares += jnp.sum((value * value).reshape(tile // 8, 8, targets_all), axis=0)

    sums[pl.ds(me, 1)] = jnp.sum(squares, axis=0, keepdims=True)[None]

    def send_sum(i):
        device = lax.rem(me + i, n)
        remote(sums.at[pl.ds(me, 1)], device, sum_send, sum_recv).start()

    each(1, n, send_sum)

    for p in range(PIECES):
        remote(piece_rows(levels, p), me, y_send.at[p], y_recv.at[0, 0, p]).wait_send()
        remote(piece_rows(2 * levels, p), me, s_send.at[p], s_recv.at[p]).wait_send()

    def z_sent(d):
        for p in range(PIECES):
            for way in range(2):

                @pl.when(jnp.logical_and(exists(way, d), onward[way][0]))
                def _():
                    ref = block(z, y, core, p)
                    remote(ref, me, z_send.at[way, d, p], z_recv.at[way, d, p]).wait_send()

    each(0, levels, z_sent)

    others = sums.at[pl.ds(0, n - 1)]
    remote(others, me, sum_send, sum_recv).wait_recv()
    power = jnp.sum(sums[...], axis=0) / (count * n)
    inverse = 1.0 / jnp.sqrt(power + 1e-06)
    for first in range(0, count, tile):
        here = slice(first, first + tile)
        out[here, :] = (raw[here, :] * inverse).astype(out.dtype)
    remote(others, me, sum_send, sum_recv).wait_send()


def shards(n, train_features, residual_weights, target_features):
    ckpts, count, depth = train_features.shape
    own = target_features.shape[1]
    dma = pltpu.SemaphoreType.DMA
    levels = n // 4
    return pl.pallas_call(
        functools.partial(kernel, n),
        out_shape=jax.ShapeDtypeStruct((count, n * own), jnp.bfloat16),
        in_specs=[pl.BlockSpec(memory_space=pl.ANY)] * 3,
        out_specs=pl.BlockSpec(memory_space=pltpu.VMEM),
        scratch_shapes=[
            pltpu.VMEM((ckpts, n * own, depth), jnp.bfloat16),
            pltpu.VMEM((ckpts, count, depth), jnp.bfloat16),
            pltpu.VMEM((ckpts, count), jnp.float32),
            pltpu.VMEM((ckpts, count, 128), jnp.float32),
            pltpu.VMEM((count, n * own), jnp.float32),
            pltpu.VMEM((n, 1, n * own), jnp.float32),
            dma, dma, dma((PIECES,)),
            dma((2, levels, PIECES)), dma((2, levels + 1, PIECES)),
            dma((PIECES,)), dma((2, levels, PIECES)),
            dma((PIECES,)), dma((PIECES,)),
            dma, dma,
        ],
        compiler_params=pltpu.CompilerParams(
            collective_id=0, has_side_effects=True, vmem_limit_bytes=56 * 1024 * 1024,
        ),
        cost_estimate=pl.CostEstimate(
            flops=2 * ckpts * count * depth * n * own,
            bytes_accessed=2 * ckpts * count * depth, transcendentals=0,
        ),
    )(train_features, residual_weights, target_features)


def solution(mesh):
    return jax.shard_map(
        functools.partial(shards, mesh.shape["trn"]),
        mesh=mesh,
        in_specs=(
            P(None, ("grp", "trn"), None),
            P(None, ("grp", "trn")),
            P(None, ("grp", "trn"), None),
        ),
        out_specs=P(("grp", "trn"), None),
        check_vma=False,
    )
```

time: 133 us -> 33.8 us (0.25)
  waiting for transfers between devices: 75.9 us -> 0 us
  Pallas kernels: 0 us -> 31.6 us
  blocking collectives: 31.6 us -> 0 us
  between operations: 13.4 us -> 0.01 us
  matrix products: 8.83 us -> 0 us
    all_gather x2 -> x0, waiting for transfers between devices: 75.2 us -> none  [shards(): lax.all_gather(target_features[ckpt], 'trn', axis=0, tiled=True)]
    pallas_call x0 -> x1, Pallas kernels: none -> 31.6 us  [shards(): pl.pallas_call(functools.partial(kernel, n), out_shape=jax.ShapeDtypeStru...]
    psum x1 -> x0, blocking collectives: 31.6 us -> none  [shards(): squares = lax.psum(jnp.sum(raw * raw, axis=0), 'trn')]
    dot_general x2 -> x0, matrix products: 8.83 us -> none  [score_one(): jnp.dot(train_features[ckpt], piece.T, preferred_element_type=jnp.float32)]
    slice x2 -> x0, local copies, waits for them, and re-layouts: 2.33 us -> none  [the longest x1 1.52 us: shards(): target_features[ckpt]]
    unnamed x0 -> x1, local copies, waits for them, and re-layouts: none -> 1.97 us
  transfers between devices with their start and end apart: 2 -> 0, of which waited for: 2 -> 0; matrix products, arithmetic and copies ran while one was open for 4% -> 0% of each run, Pallas kernels for 0% -> 0%
where the time goes in v1:
time: 33.8 us; the launch traced here: 33.6 us
  Pallas kernels  31.6 us (93%)
  local copies, waits for them, and re-layouts  1.97 us (6%)
    pallas_call x1, Pallas kernels, shards(): pl.pallas_call(functools.partial(kernel, n), out_shape=jax.ShapeDtypeStru...  31.6 us
    unnamed x1, local copies, waits for them, and re-layouts  1.97 us

profile of v1, /device:TPU:0, one launch (start us, length us, event | category | flops | bytes accessed | tf_op | source)
XLA Modules:
  0.0 33.6 jit_solution(11482810904450441842)
XLA Ops:
  0.0 31.6 %shard_map.37 = bf16[1280,256]{1,0:T(8,128)(2,1)} custom-call(bf16[2,1280,2048]{2,1,0:T(8,128)(2,1)} %train.1, f32[2,1280]{1,0:T(2,128)} %weights.1, bf16[2,16,2048]{2,1,0:T(8,128)(2,1)} %targets.1), custom_call_target="tpu_custom_call" | custom-call | flops 2684354560 | bytes 10485760 | tf_op jit(solution)/shard_map/pallas_call | solution.py:206
  31.6 2.0 %copy.5 = bf16[1280,256]{1,0:T(8,128)(2,1)} copy(bf16[1280,256]{1,0:T(8,128)(2,1)} %shard_map.37) | data formatting | bytes 1310720

commit v2 on v1

v2 whole, which is shorter than its diff:
```python
import functools

import jax
import jax.numpy as jnp
from jax import lax
from jax.experimental import pallas as pl
from jax.experimental.pallas import tpu as pltpu
from jax.sharding import PartitionSpec as P

MESH = pl.DeviceIdType.MESH
AHEAD = 2
PIECES = 2
ROW_TILE = 640


def each(low, high, body):
    if high - low <= 16:
        for i in range(low, high):
            body(i)
    else:

        @pl.loop(low, high)
        def _(i):
            body(i)


def kernel(n, train, weights, targets, out, feats, rows, weight_rows, columns, raw, sums,
           own_sem, weight_sem, load_sem, z_send, z_recv, y_send, y_recv, s_send, s_recv,
           sum_send, sum_recv):
    levels = n // 4
    me = lax.axis_index("trn")
    z, y, core = me // 4, (me // 2) % 2, me % 2
    across, sibling = z * 4 + (1 - y) * 2 + core, z * 4 + y * 2 + (1 - core)
    ckpts, count, depth = train.shape
    own = targets.shape[1]
    per_ckpt = PIECES // ckpts
    width = depth // per_ckpt
    where = [(p // per_ckpt, (p % per_ckpt) * width) for p in range(PIECES)]

    def block(zz, yy, p, size=1):
        ckpt, start = where[p]
        return feats.at[ckpt, pl.ds(zz, size), yy, core, :, pl.ds(start, width)]

    def remote(ref, device, send_sem, recv_sem):
        return pltpu.make_async_remote_copy(
            src_ref=ref, dst_ref=ref, send_sem=send_sem, recv_sem=recv_sem,
            device_id={"trn": device}, device_id_type=MESH,
        )

    own_copy = pltpu.make_async_copy(targets, feats.at[:, z, y, core], own_sem)
    own_copy.start()
    weight_copy = pltpu.make_async_copy(weights, weight_rows, weight_sem)
    weight_copy.start()
    loads = []
    for p, (ckpt, start) in enumerate(where):
        part = (ckpt, slice(None), pl.ds(start, width))
        loads.append(pltpu.make_async_copy(train.at[part], rows.at[part], load_sem.at[p]))
        loads[-1].start()

    barrier = pltpu.get_barrier_semaphore()

    def greet(device):
        pl.semaphore_signal(barrier, inc=1, device_id={"trn": device}, device_id_type=MESH)

    above, below = z + 1 < levels, z > 0
    onward = ((above, me + 4), (below, me - 4))
    greet(across)
    greet(sibling)
    for there, device in onward:
        pl.when(there)(functools.partial(greet, device))
    pl.semaphore_wait(barrier, 2 + above.astype(jnp.int32) + below.astype(jnp.int32))
    own_copy.wait()

    def pass_on(way, d, p, ref):
        there, device = onward[way]

        @pl.when(there)
        def _():
            remote(ref, device, z_send.at[way, d, p], z_recv.at[way, d + 1, p]).start()

    def to_across(p, ref):
        remote(ref, across, y_send.at[p], y_recv.at[p]).start()

    def origin(way, d):
        return z - d if way == 0 else z + d

    def exists(way, d):
        return origin(way, d) >= 0 if way == 0 else origin(way, d) < levels

    for p in range(PIECES):
        ref = block(z, y, p)
        pass_on(0, 0, p, ref)
        pass_on(1, 0, p, ref)
        to_across(p, ref)

    weight_copy.wait()
    for ckpt in range(ckpts):
        for first in range(0, count, 128):
            line = weight_rows[ckpt:ckpt + 1, first:first + 128]
            columns[ckpt, first:first + 128, :] = jnp.broadcast_to(line, (128, 128)).T

    def level(d):
        for p in range(PIECES):
            for way in range(2):

                @pl.when(exists(way, d))
                def _():
                    ref = block(origin(way, d), y, p)
                    remote(ref, me, z_send.at[way, d, p], z_recv.at[way, d, p]).wait_recv()
                    pass_on(way, d, p, ref)
                    to_across(p, ref)

    each(1, levels, level)

    def to_sibling(half, p):
        column = block(0, y if half == 0 else 1 - y, p, levels)
        if half:
            remote(column, me, y_send.at[p], y_recv.at[p]).wait_recv()
        remote(column, sibling, s_send.at[half, p], s_recv.at[half, p]).start()

    for p in range(PIECES):
        to_sibling(0, p)
    for p in range(AHEAD):
        to_sibling(1, p)

    targets_all = n * own
    tile = ROW_TILE if count % ROW_TILE == 0 else count
    lanes = targets_all // 128
    squares = jnp.zeros((8, targets_all), jnp.float32)
    for p, (ckpt, start) in enumerate(where):
        if p + AHEAD < PIECES:
            to_sibling(1, p + AHEAD)
        column = block(0, y, p, levels)
        for half in range(2):
            remote(column, me, s_send.at[half, p], s_recv.at[half, p]).wait_recv()
        loads[p].wait()
        for first in range(0, count, tile):
            here = slice(first, first + tile)
            product = lax.dot_general(
                rows[ckpt, here, start:start + width],
                feats[ckpt, :, :, :, :, start:start + width].reshape(targets_all, width),
                (((1,), (1,)), ((), ())), preferred_element_type=jnp.float32,
            )
            scale = jnp.concatenate([columns[ckpt, here, :]] * lanes, axis=1)
            value = product * scale
            if p:
                value += raw[here, :]
            raw[here, :] = value
            if p == PIECES - 1:
                squares += jnp.sum((value * value).reshape(tile // 8, 8, targets_all), axis=0)

    sums[pl.ds(me, 1)] = jnp.sum(squares, axis=0, keepdims=True)[None]

    def send_sum(i):
        device = lax.rem(me + i, n)
        remote(sums.at[pl.ds(me, 1)], device, sum_send, sum_recv).start()

    each(1, n, send_sum)

    for p in range(PIECES):
        column = block(0, y, p, levels)
        remote(column, me, y_send.at[p], y_recv.at[p]).wait_send()
        for half in range(2):
            remote(column, me, s_send.at[half, p], s_recv.at[half, p]).wait_send()

    def z_sent(d):
        for p in range(PIECES):
            for way in range(2):

                @pl.when(jnp.logical_and(exists(way, d), onward[way][0]))
                def _():
                    ref = block(z, y, p)
                    remote(ref, me, z_send.at[way, d, p], z_recv.at[way, d, p]).wait_send()

    each(0, levels, z_sent)

    others = sums.at[pl.ds(0, n - 1)]
    remote(others, me, sum_send, sum_recv).wait_recv()
    power = jnp.sum(sums[...], axis=0) / (count * n)
    inverse = 1.0 / jnp.sqrt(power + 1e-06)
    for first in range(0, count, tile):
        here = slice(first, first + tile)
        out[here, :] = (raw[here, :] * inverse).astype(out.dtype)
    remote(others, me, sum_send, sum_recv).wait_send()


def shards(n, train_features, residual_weights, target_features):
    ckpts, count, depth = train_features.shape
    own = target_features.shape[1]
    dma = pltpu.SemaphoreType.DMA
    levels = n // 4
    return pl.pallas_call(
        functools.partial(kernel, n),
        out_shape=jax.ShapeDtypeStruct((count, n * own), jnp.bfloat16),
        in_specs=[pl.BlockSpec(memory_space=pl.ANY)] * 3,
        out_specs=pl.BlockSpec(memory_space=pltpu.VMEM),
        scratch_shapes=[
            pltpu.VMEM((ckpts, levels, 2, 2, own, depth), jnp.bfloat16),
            pltpu.VMEM((ckpts, count, depth), jnp.bfloat16),
            pltpu.VMEM((ckpts, count), jnp.float32),
            pltpu.VMEM((ckpts, count, 128), jnp.float32),
            pltpu.VMEM((count, n * own), jnp.float32),
            pltpu.VMEM((n, 1, n * own), jnp.float32),
            dma, dma, dma((PIECES,)),
            dma((2, levels, PIECES)), dma((2, levels + 1, PIECES)),
            dma((PIECES,)), dma((PIECES,)),
            dma((2, PIECES)), dma((2, PIECES)),
            dma, dma,
        ],
        compiler_params=pltpu.CompilerParams(
            collective_id=0, has_side_effects=True, vmem_limit_bytes=56 * 1024 * 1024,
        ),
        cost_estimate=pl.CostEstimate(
            flops=2 * ckpts * count * depth * n * own,
            bytes_accessed=2 * ckpts * count * depth, transcendentals=0,
        ),
    )(train_features, residual_weights, target_features)


def solution(mesh):
    return jax.shard_map(
        functools.partial(shards, mesh.shape["trn"]),
        mesh=mesh,
        in_specs=(
            P(None, ("grp", "trn"), None),
            P(None, ("grp", "trn")),
            P(None, ("grp", "trn"), None),
        ),
        out_specs=P(("grp", "trn"), None),
        check_vma=False,
    )
```

time: 33.8 us -> 29.5 us (0.87)
  Pallas kernels: 31.6 us -> 27.3 us
    pallas_call x1, Pallas kernels: 31.6 us -> 27.3 us  [shards(): pl.pallas_call(functools.partial(kernel, n), out_shape=jax.ShapeDtypeStru...]
where the time goes in v2:
time: 29.5 us; the launch traced here: 29.3 us
  Pallas kernels  27.3 us (93%)
  local copies, waits for them, and re-layouts  1.97 us (7%)
    pallas_call x1, Pallas kernels, shards(): pl.pallas_call(functools.partial(kernel, n), out_shape=jax.ShapeDtypeStru...  27.3 us
    unnamed x1, local copies, waits for them, and re-layouts  1.97 us

profile of v2, /device:TPU:0, one launch (start us, length us, event | category | flops | bytes accessed | tf_op | source)
XLA Modules:
  0.0 29.3 jit_solution(2973412012865036860)
XLA Ops:
  0.0 27.3 %shard_map.37 = bf16[1280,256]{1,0:T(8,128)(2,1)} custom-call(bf16[2,1280,2048]{2,1,0:T(8,128)(2,1)} %train.1, f32[2,1280]{1,0:T(2,128)} %weights.1, bf16[2,16,2048]{2,1,0:T(8,128)(2,1)} %targets.1), custom_call_target="tpu_custom_call" | custom-call | flops 2684354560 | bytes 10485760 | tf_op jit(solution)/shard_map/pallas_call | solution.py:192
  27.3 2.0 %copy.5 = bf16[1280,256]{1,0:T(8,128)(2,1)} copy(bf16[1280,256]{1,0:T(8,128)(2,1)} %shard_map.37) | data formatting | bytes 1310720

commit v3 on v2

--- a/solution.py
+++ b/solution.py
@@ -191,7 +191,7 @@
     levels = n // 4
     return pl.pallas_call(
         functools.partial(kernel, n),
-        out_shape=jax.ShapeDtypeStruct((count, n * own), jnp.bfloat16),
+        out_shape=pltpu.VMEM((count, n * own), jnp.bfloat16),
         in_specs=[pl.BlockSpec(memory_space=pl.ANY)] * 3,
         out_specs=pl.BlockSpec(memory_space=pltpu.VMEM),
         scratch_shapes=[

time: 29.5 us -> 27.5 us (0.932)
  local copies, waits for them, and re-layouts: 1.97 us -> 0.84 us
  Pallas kernels: 27.3 us -> 26.5 us
    unnamed x1, local copies, waits for them, and re-layouts: 1.97 us -> 0.84 us
    pallas_call x1, Pallas kernels: 27.3 us -> 26.5 us  [shards(): pl.pallas_call(functools.partial(kernel, n), out_shape=pltpu.VMEM((count,...]
where the time goes in v3:
time: 27.5 us; the launch traced here: 27.3 us
  Pallas kernels  26.5 us (96%)
  local copies, waits for them, and re-layouts  0.84 us (3%)
    pallas_call x1, Pallas kernels, shards(): pl.pallas_call(functools.partial(kernel, n), out_shape=pltpu.VMEM((count,...  26.5 us
    unnamed x1, local copies, waits for them, and re-layouts  0.84 us

profile of v3, /device:TPU:0, one launch (start us, length us, event | category | flops | bytes accessed | tf_op | source)
XLA Modules:
  0.0 27.3 jit_solution(14243442848547024854)
XLA Ops:
  0.0 26.5 %shard_map.37 = bf16[1280,256]{1,0:T(8,128)(2,1)S(1)} custom-call(bf16[2,1280,2048]{2,1,0:T(8,128)(2,1)} %train.1, f32[2,1280]{1,0:T(2,128)} %weights.1, bf16[2,16,2048]{2,1,0:T(8,128)(2,1)} %targets.1), custom_call_target="tpu_custom_call" | custom-call | flops 2684354560 | bytes 10485760 | tf_op jit(solution)/shard_map/pallas_call | solution.py:192
  26.5 0.8 %copy.5 = bf16[1280,256]{1,0:T(8,128)(2,1)} copy(bf16[1280,256]{1,0:T(8,128)(2,1)S(1)} %shard_map.37) | data formatting | bytes 1310720
